TPU v7x, 256 devices: a whole 4x4x8 slice. The times are simulated.
256 devices in a mesh: ta: 16 (over x_lo, z), gz: 2 (over core), gy: 4 (over y), gx: 2 (over x_hi).
Axes of the slice: x: 4 (x_hi: 2, x_lo: 2; x = x_hi * 2 + x_lo), y: 4, z: 8, core: 2. Of those that a mesh axis runs over, the one named last changes fastest.
Arguments:
- source: float32 [2, 4, 3, 16, 2, 4, 8, 256], P(None, None, None, 'ta', 'gz', 'gy', 'gx'), may hold values from -6 to 6
- gauge_links: bfloat16 [4, 2, 3, 3, 16, 2, 4, 8, 256], P(None, None, None, None, 'ta', 'gz', 'gy', 'gx'), may hold values from -2.5 to 2.5
- clover_inverse: bfloat16 [2, 2, 6, 6, 16, 2, 4, 8, 256], P(None, None, None, None, 'ta', 'gz', 'gy', 'gx'), may hold values from -0.5 to 1.5, as said below
- vectors: bfloat16 [16, 2, 4, 3, 16, 2, 4, 8, 256], P(None, None, None, None, 'ta', 'gz', 'gy', 'gx'), may hold values from -0.75 to 0.75
- coarse_hops: float32 [8, 2, 16, 16, 16, 2, 4, 8], P(None, None, None, None, 'ta', 'gz', 'gy', 'gx'), may hold values from -0.25 to 0.25
Outputs:
- solution: float32 [2, 4, 3, 16, 2, 4, 8, 256], P(None, None, None, 'ta', 'gz', 'gy', 'gx')
- coarse_error: float32 [2, 16, 16, 2, 4, 8], P(None, None, 'ta', 'gz', 'gy', 'gx')
Inputs may be any that keep to these rules, and one draw needn't show every extreme that they name: `clover_inverse`: each chirality block is hermitian.
All inputs are finite; a program needn't handle non-finite values.
Results may differ from a plain program's by a relative error of at most 0.0029.
Values sent between devices are 32-bit elements; how exact they have to be, the bound alone decides.
A program may use at most 128 MiB of HBM per device.

v0:
```python
import jax
import jax.numpy as jnp
from jax import lax
from jax.experimental import pallas as pl
from jax.experimental.pallas import tpu as pltpu
from jax.sharding import PartitionSpec as P


kappa_value = 0.125
fine_relax = 0.8
coarse_relax = 0.7

F32 = jnp.float32
BF16 = jnp.bfloat16

B_ROWS = (((0, 0), (1, 0)), ((0, 3), (1, 1)), ((1, 2), (0, 0)), ((1, 3), (0, 3)))
B_ADJOINT_ROWS = (((0, 0), (1, 0)), ((0, 1), (1, 3)), ((1, 0), (0, 2)), ((1, 1), (0, 1)))

T_AHEAD, T_BEHIND, Y_AHEAD, Y_BEHIND, Z_BOTH, X_BOTH = 0, 3, 6, 9, 12, 18
TILES = 21


def plus_unit(target, unit, value):
    if unit == 0:
        return target[0] + value[0], target[1] + value[1]
    if unit == 1:
        return target[0] - value[1], target[1] + value[0]
    if unit == 2:
        return target[0] - value[0], target[1] - value[1]
    return target[0] + value[1], target[1] - value[0]


def project(spins, direction, sign):
    halves = []
    for row in range(2):
        column, unit = B_ROWS[direction][row]
        unit = unit if sign > 0 else (unit + 2) % 4
        halves.append(plus_unit(spins[row], unit, spins[2 + column]))
    return jnp.concatenate([halves[0][0], halves[1][0], halves[0][1], halves[1][1]], axis=0)


def lift(summed, half, direction, sign):
    pair = [(half[0:3], half[6:9]), (half[3:6], half[9:12])]
    result = []
    for row in range(2):
        result.append(plus_unit(summed[row], 0, pair[row]))
    for row in range(2):
        column, unit = B_ADJOINT_ROWS[direction][row]
        unit = unit if sign > 0 else (unit + 2) % 4
        result.append(plus_unit(summed[2 + row], unit, pair[column]))
    return result


def link_times(links, direction, half, dagger):
    real_part = half[:6].reshape(2, 3, 8, 128)
    imag_part = half[6:].reshape(2, 3, 8, 128)
    out_real = out_imag = None
    for b in range(3):
        if dagger:
            u_real, u_imag = links[direction, 0, b], links[direction, 1, b]
        else:
            u_real, u_imag = links[direction, 0, :, b], links[direction, 1, :, b]
        u_real, u_imag = u_real[None], u_imag[None]
        v_real, v_imag = real_part[:, b][:, None], imag_part[:, b][:, None]
        if dagger:
            term_real = u_real * v_real + u_imag * v_imag
            term_imag = u_real * v_imag - u_imag * v_real
        else:
            term_real = u_real * v_real - u_imag * v_imag
            term_imag = u_real * v_imag + u_imag * v_real
        out_real = term_real if out_real is None else out_real + term_real
        out_imag = term_imag if out_imag is None else out_imag + term_imag
    return jnp.concatenate([out_real.reshape(6, 8, 128), out_imag.reshape(6, 8, 128)], axis=0)


def lane_roll(values, shift):
    shift = shift % 128
    return values if shift == 0 else pltpu.roll(values, shift, values.ndim - 1)


def row_roll(values, shift):
    shift = shift % 8
    return values if shift == 0 else pltpu.roll(values, shift, values.ndim - 2)


class Places:
    def __init__(self):
        row = lax.broadcasted_iota(jnp.int32, (8, 128), 0)
        lane = lax.broadcasted_iota(jnp.int32, (8, 128), 1)
        self.row, self.lane = row, lane
        self.block = row % 4
        self.half = row // 4
        self.parity = lane // 64
        self.slot = {1: (lane // 16) % 4, 2: (lane // 4) % 4, 3: lane % 4}


STRIDE = {1: 16, 2: 4, 3: 1}


def choose(mask, first, second):
    return jnp.where(jnp.broadcast_to(mask[None], first.shape), first, second)


def pack_slots(half, direction, ahead, places):
    stride, slot = STRIDE[direction], places.slot[direction]
    fours = half.reshape(3, 4, 8, 128)
    packed = fours[:, 0]
    for k in range(1, 4):
        if ahead:
            packed = choose(slot == k, lane_roll(fours[:, k], stride * k), packed)
        else:
            packed = choose(slot == 3 - k, lane_roll(fours[:, k], -stride * k), packed)
    return packed


def merge_slots(rolled, packed, direction, ahead, places):
    stride, slot = STRIDE[direction], places.slot[direction]
    fours = rolled.reshape(3, 4, 8, 128)
    merged = []
    for k in range(4):
        if ahead:
            merged.append(choose(slot == 3, lane_roll(packed, stride * (3 - k)), fours[:, k]))
        else:
            merged.append(choose(slot == 0, lane_roll(packed, -stride * (3 - k)), fours[:, k]))
    return jnp.stack(merged, axis=1).reshape(12, 8, 128)


def pack_time(half, ahead, places):
    edge = places.parity == (0 if ahead else 1)
    edge_rows = places.half == (0 if ahead else 1)
    pairs = half.reshape(6, 2, 8, 128)
    first, second = pairs[:, 0], lane_roll(pairs[:, 1], 64)
    paired = choose(edge, first, second).reshape(3, 2, 8, 128)
    paired_first, paired_second = paired[:, 0], row_roll(paired[:, 1], 4)
    packed = choose(edge_rows, paired_first, paired_second)
    return packed, (first, second, paired_first, paired_second)


def merge_time(state, packed, ahead, places):
    edge = places.parity == (0 if ahead else 1)
    edge_rows = places.half == (0 if ahead else 1)
    first, second, paired_first, paired_second = state
    next_first = row_roll(choose(edge_rows, packed, paired_first), 4)
    next_second = choose(edge_rows, paired_second, packed)
    moved = jnp.stack([next_first, next_second], axis=1).reshape(6, 8, 128)
    out_first = lane_roll(choose(edge, moved, first), 64)
    out_second = choose(edge, second, moved)
    return jnp.stack([out_first, out_second], axis=1).reshape(12, 8, 128)


def spins_of(values):
    return [(values[3 * s : 3 * s + 3], values[12 + 3 * s : 15 + 3 * s]) for s in range(4)]


def tiles_of(spins):
    return jnp.concatenate([spin[0] for spin in spins] + [spin[1] for spin in spins], axis=0)


def kernel(
    source_hbm,
    links_hbm,
    clover_hbm,
    vectors_hbm,
    hops_hbm,
    out_ref,
    coarse_ref,
    source_ref,
    links_raw,
    clover_raw,
    vectors_raw,
    hops_ref,
    links,
    clover,
    wide,
    faces,
    scaled,
    send_buffer,
    recv_buffer,
    coarse_send,
    coarse_recv,
    load_sem,
    send_sem,
    recv_sem,
    coarse_send_sem,
    coarse_recv_sem,
):
    loads = []
    for index, (origin, target) in enumerate(
        (
            (source_hbm, source_ref),
            (links_hbm, links_raw),
            (clover_hbm, clover_raw),
            (vectors_hbm, vectors_raw),
            (hops_hbm, hops_ref),
        )
    ):
        loads.append(pltpu.make_async_copy(origin, target, load_sem.at[index]))

    def around(axis, step):
        count = lax.axis_size(axis)
        return {axis: lax.rem(lax.axis_index(axis) + (step + count), count)}

    t_next, t_prior = around("ta", 1), around("ta", -1)
    y_next, y_prior = around("gy", 1), around("gy", -1)
    z_other, x_other = around("gz", 1), around("gx", 1)

    barrier = pltpu.get_barrier_semaphore()
    for neighbour in (x_other, t_next, t_prior, y_next, y_prior, z_other):
        pl.semaphore_signal(
            barrier, inc=1, device_id=neighbour, device_id_type=pl.DeviceIdType.MESH
        )

    loads[0].start()
    loads[1].start()
    places = Places()

    def message(sweep, number, start, count, target):
        window = pl.ds(start, count)
        return pltpu.make_async_remote_copy(
            src_ref=send_buffer.at[sweep, window],
            dst_ref=recv_buffer.at[sweep, window],
            send_sem=send_sem.at[sweep, number],
            recv_sem=recv_sem.at[sweep, number],
            device_id=target,
            device_id_type=pl.DeviceIdType.MESH,
        )

    started = []

    def settle(keep):
        while len(started) > keep:
            started.pop(0).wait_send()

    def clover_hopping(sweep, psi, before_send=None, while_waiting=None, sent=()):
        spins = spins_of(psi)
        send = send_buffer.at[sweep]
        recv = recv_buffer.at[sweep]
        ahead, behind, messages = {}, {}, {}

        def halves(mu):
            ahead[mu] = project(spins, mu, -1)
            behind[mu] = link_times(links, mu, project(spins, mu, 1), True)

        def dispatch(number, start, count, target):
            if number in sent:
                messages[number] = sent[number]
                return
            messages[number] = message(sweep, number, start, count, target)
            started.append(messages[number])
            if before_send is None:
                messages[number].start()

        halves(3)
        x_ahead = pack_slots(ahead[3], 3, True, places)
        x_behind = pack_slots(behind[3], 3, False, places)
        if 0 not in sent:
            send[X_BOTH : X_BOTH + 3] = choose(places.block == 0, x_ahead, x_behind)
        dispatch(0, X_BOTH, 3, x_other)
        ahead[0] = project(spins, 0, -1)
        t_ahead, t_ahead_state = pack_time(ahead[0], True, places)
        if 1 not in sent:
            send[T_AHEAD : T_AHEAD + 3] = t_ahead
        dispatch(1, T_AHEAD, 3, t_prior)
        behind[0] = link_times(links, 0, project(spins, 0, 1), True)
        t_behind, t_behind_state = pack_time(behind[0], False, places)
        if 2 not in sent:
            send[T_BEHIND : T_BEHIND + 3] = t_behind
        dispatch(2, T_BEHIND, 3, t_next)
        halves(2)
        send[Y_AHEAD : Y_AHEAD + 3] = pack_slots(ahead[2], 2, True, places)
        dispatch(3, Y_AHEAD, 3, y_prior)
        send[Y_BEHIND : Y_BEHIND + 3] = pack_slots(behind[2], 2, False, places)
        dispatch(4, Y_BEHIND, 3, y_next)
        halves(1)
        send[Z_BOTH : Z_BOTH + 3] = pack_slots(ahead[1], 1, True, places)
        send[Z_BOTH + 3 : Z_BOTH + 6] = pack_slots(behind[1], 1, False, places)
        dispatch(5, Z_BOTH, 6, z_other)
        if before_send is not None:
            before_send()
            for copy in messages.values():
                copy.start()
        settle(6)
        if while_waiting is not None:
            while_waiting()

        ahead_moved = {mu: lane_roll(ahead[mu], -STRIDE[mu]) for mu in (1, 2, 3)}
        behind_moved = {mu: lane_roll(behind[mu], STRIDE[mu]) for mu in (1, 2, 3)}
        zero = jnp.zeros((3, 8, 128), F32)
        summed = [(zero, zero)] * 4

        def finish(summed, mu, from_ahead, from_behind):
            summed = lift(summed, link_times(links, mu, from_ahead, False), mu, -1)
            return lift(summed, from_behind, mu, 1)

        messages[5].wait_recv()
        summed = finish(
            summed,
            1,
            merge_slots(ahead_moved[1], recv[Z_BOTH : Z_BOTH + 3], 1, True, places),
            merge_slots(behind_moved[1], recv[Z_BOTH + 3 : Z_BOTH + 6], 1, False, places),
        )
        messages[3].wait_recv()
        messages[4].wait_recv()
        summed = finish(
            summed,
            2,
            merge_slots(ahead_moved[2], recv[Y_AHEAD : Y_AHEAD + 3], 2, True, places),
            merge_slots(behind_moved[2], recv[Y_BEHIND : Y_BEHIND + 3], 2, False, places),
        )
        messages[0].wait_recv()
        x_recv = recv[X_BOTH : X_BOTH + 3]
        x_from_ahead = choose(places.block == 3, row_roll(x_recv, 3), row_roll(x_ahead, -1))
        x_from_behind = choose(places.block == 0, row_roll(x_recv, -3), row_roll(x_behind, 1))
        summed = finish(
            summed,
            3,
            merge_slots(ahead_moved[3], x_from_ahead, 3, True, places),
            merge_slots(behind_moved[3], x_from_behind, 3, False, places),
        )
        messages[1].wait_recv()
        messages[2].wait_recv()
        summed = finish(
            summed,
            0,
            merge_time(t_ahead_state, recv[T_AHEAD : T_AHEAD + 3], True, places),
            merge_time(t_behind_state, recv[T_BEHIND : T_BEHIND + 3], False, places),
        )

        result = []
        for chirality in range(2):
            pair = summed[2 * chirality : 2 * chirality + 2]
            out_real = out_imag = None
            for column in range(6):
                c_real = clover[chirality, 0, :, column]
                c_imag = clover[chirality, 1, :, column]
                v_real = pair[column // 3][0][column % 3][None]
                v_imag = pair[column // 3][1][column % 3][None]
                term_real = c_real * v_real - c_imag * v_imag
                term_imag = c_real * v_imag + c_imag * v_real
                out_real = term_real if out_real is None else out_real + term_real
                out_imag = term_imag if out_imag is None else out_imag + term_imag
            result.append((out_real[:3], out_imag[:3]))
            result.append((out_real[3:], out_imag[3:]))
        return tiles_of(result)

    loads[0].wait()
    scaled[...] = fine_relax * source_ref[...]

    def prepare():
        loads[2].wait()
        clover[...] = (fine_relax * kappa_value) * clover_raw[...].astype(F32).reshape(clover.shape)
        loads[3].wait()
        wide[...] = vectors_raw[...].astype(F32).reshape(wide.shape)

    def vector_faces():
        def four(step, carry):
            for k in range(4):
                k = 4 * step + k
                spins = spins_of(wide[k].reshape(24, 8, 128))
                halves = [
                    project(spins, 3, -1),
                    link_times(links, 3, project(spins, 3, 1), True),
                    project(spins, 0, -1),
                    link_times(links, 0, project(spins, 0, 1), True),
                ]
                for part in range(2):
                    if part == 1:
                        halves = [
                            jnp.concatenate([-half[6:], half[:6]], axis=0) for half in halves
                        ]
                    faces[k, part, 0:3] = choose(
                        places.block == 0,
                        pack_slots(halves[0], 3, True, places),
                        pack_slots(halves[1], 3, False, places),
                    )
                    faces[k, part, 3:6] = pack_time(halves[2], True, places)[0]
                    faces[k, part, 6:9] = pack_time(halves[3], False, places)[0]
            return carry

        lax.fori_loop(0, 4, four, 0)

    def enter():
        pl.semaphore_wait(barrier, 6)

    loads[1].wait()
    for load in loads[2:]:
        load.start()
    links[...] = links_raw[...].astype(F32).reshape(links.shape)

    psi = scaled[...]
    psi = (1.0 - fine_relax) * psi + scaled[...] + clover_hopping(0, psi, enter, prepare)

    change = clover_hopping(1, psi, None, vector_faces)
    residual = source_ref[...] - psi + (1.0 / fine_relax) * change

    rounded = residual.astype(BF16).astype(F32)
    rest_real, rest_imag = rounded[:12], rounded[12:]
    reals, imags = [], []
    for k in range(16):
        v_real, v_imag = wide[k, 0], wide[k, 1]
        reals.append(jnp.sum(v_real * rest_real + v_imag * rest_imag, axis=0))
        imags.append(jnp.sum(v_real * rest_imag - v_imag * rest_real, axis=0))

    def over_lanes(tile):
        return jnp.broadcast_to(jnp.sum(tile, axis=-1, keepdims=True), (8, 128))

    def into_lanes(columns):
        layer = list(columns)
        bit = 1
        while len(layer) > 1:
            odd = (places.lane // bit) % 2 == 1
            layer = [
                jnp.where(odd, layer[n + 1], layer[n]) for n in range(0, len(layer), 2)
            ]
            bit *= 2
        return layer[0]

    reals = [over_lanes(tile) for tile in reals]
    imags = [over_lanes(tile) for tile in imags]
    coarse_real, coarse_imag = into_lanes(reals), into_lanes(imags)
    coarse_real = coarse_real + row_roll(coarse_real, 4)
    coarse_imag = coarse_imag + row_roll(coarse_imag, 4)

    own = jnp.where(places.half == 0, coarse_real, coarse_imag)
    coarse_send[...] = own
    coarse_messages = {}
    for number, target in ((1, t_prior), (2, t_next), (0, x_other), (3, y_prior), (4, y_next), (5, z_other)):
        copy = pltpu.make_async_remote_copy(
            src_ref=coarse_send,
            dst_ref=coarse_recv.at[number],
            send_sem=coarse_send_sem.at[number],
            recv_sem=coarse_recv_sem.at[number],
            device_id=target,
            device_id_type=pl.DeviceIdType.MESH,
        )
        copy.start()
        coarse_messages[number] = copy
        started.append(copy)
    settle(6)

    def before_neighbours(total):
        value = total + row_roll(total, 4)
        first = coarse_relax * value
        return first + coarse_relax * (value - first)

    real_bases = [before_neighbours(total) for total in reals]
    imag_bases = [before_neighbours(total) for total in imags]
    loads[4].wait()

    accumulated = [jnp.zeros((8, 8, 16), F32), jnp.zeros((8, 8, 16), F32)]

    def add_hop(number, tile):
        tile = coarse_relax * tile
        swapped = row_roll(tile, 4)
        e_real = jnp.where(places.half == 0, tile, swapped)[:, :16][None]
        e_imag = jnp.where(places.half == 0, swapped, tile)[:, :16][None]
        h_real, h_imag = hops_ref[number, 0], hops_ref[number, 1]
        accumulated[0] = accumulated[0] + (h_real * e_real - h_imag * e_imag)
        accumulated[1] = accumulated[1] + (h_real * e_imag + h_imag * e_real)

    coarse_messages[5].wait_recv()
    z_tile = coarse_recv[5]
    add_hop(2, z_tile)
    add_hop(3, z_tile)
    coarse_messages[3].wait_recv()
    add_hop(4, coarse_recv[3])
    coarse_messages[4].wait_recv()
    add_hop(5, coarse_recv[4])
    coarse_messages[0].wait_recv()
    x_tile = coarse_recv[0]
    add_hop(6, jnp.where(places.block == 3, row_roll(x_tile, 3), row_roll(own, -1)))
    add_hop(7, jnp.where(places.block == 0, row_roll(x_tile, -3), row_roll(own, 1)))
    coarse_messages[1].wait_recv()
    add_hop(0, coarse_recv[1])
    coarse_messages[2].wait_recv()
    add_hop(1, coarse_recv[2])

    def errors(bases, values):
        spread = []
        for pair in range(8):
            total = jnp.broadcast_to(
                jnp.sum(values[pair], axis=-1, keepdims=True), (8, 128)
            )
            swapped = row_roll(total, 4)
            spread.append(jnp.where(places.half == 0, total, swapped))
            spread.append(jnp.where(places.half == 0, swapped, total))
        return [bases[k] + coarse_relax * spread[k] for k in range(16)]

    exact_real = errors(real_bases, accumulated[0])
    exact_imag = errors(imag_bases, accumulated[1])

    error_real = [error.astype(BF16).astype(F32) for error in exact_real]
    error_imag = [error.astype(BF16).astype(F32) for error in exact_imag]

    sent = {}
    for number, place, start, target in (
        (0, 0, X_BOTH, x_other),
        (1, 3, T_AHEAD, t_prior),
        (2, 6, T_BEHIND, t_next),
    ):
        face = send_buffer[1, start : start + 3]
        for k in range(16):
            face = face + (
                error_real[k][None] * faces[k, 0, place : place + 3]
                + error_imag[k][None] * faces[k, 1, place : place + 3]
            )
        send_buffer[2, start : start + 3] = face
        sent[number] = message(2, number, start, 3, target)
        sent[number].start()
        started.append(sent[number])

    add_real, add_imag = psi[:12], psi[12:]
    for k in range(16):
        v_real, v_imag = wide[k, 0], wide[k, 1]
        e_real, e_imag = error_real[k][None], error_imag[k][None]
        add_real = add_real + (v_real * e_real - v_imag * e_imag)
        add_imag = add_imag + (v_real * e_imag + v_imag * e_real)
    psi = jnp.concatenate([add_real, add_imag], axis=0)

    def hand_out():
        coarse_ref[0] = into_lanes(exact_real)[:4, :16]
        coarse_ref[1] = into_lanes(exact_imag)[:4, :16]

    for sweep in (2, 3):
        psi = (
            (1.0 - fine_relax) * psi
            + scaled[...]
            + clover_hopping(
                sweep, psi, None, hand_out if sweep == 2 else None, sent if sweep == 2 else ()
            )
        )
    out_ref[...] = psi

    settle(0)


def deliver(out_in, coarse_in, out_ref, coarse_ref, sems):
    copies = [
        pltpu.make_async_copy(out_in, out_ref, sems.at[0]),
        pltpu.make_async_copy(coarse_in, coarse_ref, sems.at[1]),
    ]
    for copy in copies:
        copy.start()
    for copy in copies:
        copy.wait()


def rows_of_eight(values):
    count = values.size // 1024
    return values.reshape(count, 4, 2, 128).transpose(0, 2, 1, 3).reshape(count, 8, 128)


def local(source, gauge_links, clover_inverse, vectors, coarse_hops):
    source_tiles = rows_of_eight(source)
    link_tiles = rows_of_eight(gauge_links).reshape(36, 16, 128)
    clover_tiles = rows_of_eight(clover_inverse).reshape(72, 16, 128)
    vector_tiles = rows_of_eight(vectors).reshape(32, 6, 16, 128)
    hop_tiles = (
        coarse_hops.reshape(8, 2, 16, 16, 4).transpose(0, 1, 2, 4, 3).reshape(8, 2, 8, 8, 16)
    )
    out, coarse = pl.pallas_call(
        kernel,
        out_shape=(
            jax.ShapeDtypeStruct((24, 8, 128), F32),
            jax.ShapeDtypeStruct((2, 4, 16), F32),
        ),
        in_specs=[pl.BlockSpec(memory_space=pltpu.HBM)] * 5,
        out_specs=(
            pl.BlockSpec(memory_space=pltpu.VMEM),
            pl.BlockSpec(memory_space=pltpu.VMEM),
        ),
        scratch_shapes=[
            pltpu.VMEM((24, 8, 128), F32),
            pltpu.VMEM((36, 16, 128), BF16),
            pltpu.VMEM((72, 16, 128), BF16),
            pltpu.VMEM((32, 6, 16, 128), BF16),
            pltpu.VMEM((8, 2, 8, 8, 16), F32),
            pltpu.VMEM((4, 2, 3, 3, 8, 128), F32),
            pltpu.VMEM((2, 2, 6, 6, 8, 128), F32),
            pltpu.VMEM((16, 2, 12, 8, 128), F32),
            pltpu.VMEM((16, 2, 9, 8, 128), F32),
            pltpu.VMEM((24, 8, 128), F32),
            pltpu.VMEM((4, TILES, 8, 128), F32),
            pltpu.VMEM((4, TILES, 8, 128), F32),
            pltpu.VMEM((8, 128), F32),
            pltpu.VMEM((6, 8, 128), F32),
            pltpu.SemaphoreType.DMA((5,)),
            pltpu.SemaphoreType.DMA((4, 6)),
            pltpu.SemaphoreType.DMA((4, 6)),
            pltpu.SemaphoreType.DMA((6,)),
            pltpu.SemaphoreType.DMA((6,)),
        ],
        compiler_params=pltpu.CompilerParams(
            collective_id=0, has_side_effects=True, vmem_limit_bytes=55040 * 1024
        ),
    )(source_tiles, link_tiles, clover_tiles, vector_tiles, hop_tiles)
    out, coarse = pl.pallas_call(
        deliver,
        out_shape=(
            jax.ShapeDtypeStruct((24, 8, 128), F32),
            jax.ShapeDtypeStruct((2, 4, 16), F32),
        ),
        in_specs=[pl.BlockSpec(memory_space=pl.ANY)] * 2,
        out_specs=[pl.BlockSpec(memory_space=pl.ANY)] * 2,
        scratch_shapes=[pltpu.SemaphoreType.DMA((2,))],
        compiler_params=pltpu.CompilerParams(vmem_limit_bytes=1024 * 1024),
    )(out, coarse)
    solution_out = (
        out.reshape(24, 2, 4, 128).transpose(0, 2, 1, 3).reshape(2, 4, 3, 1, 1, 1, 4, 256)
    )
    coarse_out = coarse.transpose(0, 2, 1).reshape(2, 16, 1, 1, 1, 4)
    return solution_out, coarse_out


def solution(mesh):
    return jax.shard_map(
        local,
        mesh=mesh,
        in_specs=(
            P(None, None, None, "ta", "gz", "gy", "gx", None),
            P(None, None, None, None, "ta", "gz", "gy", "gx", None),
            P(None, None, None, None, "ta", "gz", "gy", "gx", None),
            P(None, None, None, None, "ta", "gz", "gy", "gx", None),
            P(None, None, None, None, "ta", "gz", "gy", "gx"),
        ),
        out_specs=(
            P(None, None, None, "ta", "gz", "gy", "gx", None),
            P(None, None, "ta", "gz", "gy", "gx"),
        ),
        check_vma=False,
    )
```

profile of v0, /device:TPU:24, one launch (start us, length us, event | category | flops | bytes accessed | tf_op | source)
XLA Modules:
  0.0 30.0 jit_solution(8884144149793020628)
XLA Ops:
  0.6 28.7 %shard_map.68 = (f32[24,8,128]{2,1,0:T(8,128)S(1)}, f32[2,4,16]{2,1,0:T(4,128)S(1)}) custom-call(f32[24,8,128]{2,1,0:T(8,128)} %bitcast.37, bf16[36,16,128]{2,1,0:T(8,128)(2,1)} %bitcast.36, bf16[72,16,128]{2,1,0:T(8,128)(2,1)} %bitcast.35, bf16[32,6,16,128]{3,2,1,0:T(8,128)(2,1)} %bitcast.33, f32[8,2,8,8,16]{4,3,2,1,0:T(8,128)} %bitcast.34), custom_call_target="tpu_custom_call" | custom-call | tf_op jit(solution)/shard_map/pallas_call | solution.py:561
  29.3 0.7 %shard_map.69 = (f32[24,8,128]{2,1,0:T(8,128)}, f32[2,4,16]{2,1,0:T(4,128)}) custom-call(f32[24,8,128]{2,1,0:T(8,128)S(1)} %get-tuple-element.6.out_in, f32[2,4,16]{2,1,0:T(4,128)S(1)} %get-tuple-element.7.coarse_in), custom_call_target="tpu_custom_call" | custom-call | tf_op jit(solution)/shard_map/pallas_call | solution.py:597
where the time goes:
time: 30.5 us; the launch traced here: 30 us
  Pallas kernels  29.3 us (96%)
  between operations  0.64 us (2%)
    pallas_call x1, Pallas kernels, local(): pl.pallas_call(kernel, out_shape=(jax.ShapeDtypeStruct((24, 8, 128), F32)...  28.7 us
    pallas_call x1, Pallas kernels, local(): pl.pallas_call(deliver, out_shape=(jax.ShapeDtypeStruct((24, 8, 128), F32...  0.66 us

commit v1 on v0

--- a/solution.py
+++ b/solution.py
@@ -351,8 +351,9 @@
         clover[...] = (fine_relax * kappa_value) * clover_raw[...].astype(F32).reshape(clover.shape)
         loads[3].wait()
         wide[...] = vectors_raw[...].astype(F32).reshape(wide.shape)
-
-    def vector_faces():
+        vector_faces(0, 2)
+
+    def vector_faces(begin, end):
         def four(step, carry):
             for k in range(4):
                 k = 4 * step + k
@@ -377,7 +378,7 @@
                     faces[k, part, 6:9] = pack_time(halves[3], False, places)[0]
             return carry
 
-        lax.fori_loop(0, 4, four, 0)
+        lax.fori_loop(begin, end, four, 0)
 
     def enter():
         pl.semaphore_wait(barrier, 6)
@@ -390,7 +391,7 @@
     psi = scaled[...]
     psi = (1.0 - fine_relax) * psi + scaled[...] + clover_hopping(0, psi, enter, prepare)
 
-    change = clover_hopping(1, psi, None, vector_faces)
+    change = clover_hopping(1, psi, None, lambda: vector_faces(2, 4))
     residual = source_ref[...] - psi + (1.0 / fine_relax) * change
 
     rounded = residual.astype(BF16).astype(F32)

time: 30.5 us -> 30.5 us (level)
  no operation moved by 1% of the time
where the time goes in v1:
time: 30.5 us; the launch traced here: 30 us
  Pallas kernels  29.3 us (96%)
  between operations  0.64 us (2%)
    pallas_call x1, Pallas kernels, local(): pl.pallas_call(kernel, out_shape=(jax.ShapeDtypeStruct((24, 8, 128), F32)...  28.7 us
    pallas_call x1, Pallas kernels, local(): pl.pallas_call(deliver, out_shape=(jax.ShapeDtypeStruct((24, 8, 128), F32...  0.66 us

profile of v1, /device:TPU:24, one launch (start us, length us, event | category | flops | bytes accessed | tf_op | source)
XLA Modules:
  0.0 30.0 jit_solution(13395985186681737384)
XLA Ops:
  0.6 28.7 %shard_map.68 = (f32[24,8,128]{2,1,0:T(8,128)S(1)}, f32[2,4,16]{2,1,0:T(4,128)S(1)}) custom-call(f32[24,8,128]{2,1,0:T(8,128)} %bitcast.37, bf16[36,16,128]{2,1,0:T(8,128)(2,1)} %bitcast.36, bf16[72,16,128]{2,1,0:T(8,128)(2,1)} %bitcast.35, bf16[32,6,16,128]{3,2,1,0:T(8,128)(2,1)} %bitcast.33, f32[8,2,8,8,16]{4,3,2,1,0:T(8,128)} %bitcast.34), custom_call_target="tpu_custom_call" | custom-call | tf_op jit(solution)/shard_map/pallas_call | solution.py:562
  29.3 0.7 %shard_map.69 = (f32[24,8,128]{2,1,0:T(8,128)}, f32[2,4,16]{2,1,0:T(4,128)}) custom-call(f32[24,8,128]{2,1,0:T(8,128)S(1)} %get-tuple-element.6.out_in, f32[2,4,16]{2,1,0:T(4,128)S(1)} %get-tuple-element.7.coarse_in), custom_call_target="tpu_custom_call" | custom-call | tf_op jit(solution)/shard_map/pallas_call | solution.py:598
